TPU v7x, 256 devices: a whole 4x4x8 slice. The times are simulated.
256 devices in a mesh: lat: 32 (over y_lo, z, core), lon: 8 (over y_hi, x).
Axes of the slice: x: 4, y: 4 (y_hi: 2, y_lo: 2; y = y_hi * 2 + y_lo), z: 8, core: 2. Of those that a mesh axis runs over, the one named last changes fastest.
Arguments:
- cotangent: bfloat16 [384, 384, 1024], P(None, 'lat', 'lon'), may hold values from -6 to 6
- layer_input: bfloat16 [384, 384, 1024], P(None, 'lat', 'lon'), may hold values from -6 to 6
- filter_values: bfloat16 [3, 384, 4, 17], replicated, may hold values from -4 to 4
- weights: bfloat16 [3, 384, 384], replicated, may hold values from -0.1875 to 0.1875
- row_offset: int32 [384], replicated, may hold values from -3 to 0, as said below
- reach: int32 [384], replicated, may hold values from 1 to 9, as said below
Outputs:
- input_grad: bfloat16 [384, 384, 1024], P(None, 'lat', 'lon')
- weight_grad: float32 [3, 384, 384], replicated
Inputs may be any that keep to these rules, and one draw needn't show every extreme that they name: The support rows of output latitude o are o + row_offset[o] to o + row_offset[o] + 3. Taps d with |d| < reach[o] are used.
All inputs are finite; a program needn't handle non-finite values.
Results may differ from a plain program's by a relative error of at most 0.0049.
Values may be sent and summed in bfloat16 or wider, within the bound.
A program may use at most 128 MiB of HBM per device.

v0:
```python
import jax
import jax.numpy as jnp
from jax import lax
from jax.sharding import PartitionSpec as P


def with_halo(x, sides, width):
    for axis, dim in sides:
        devices, length = (lax.axis_size(axis), x.shape[dim])
        up = [(i, (i + 1) % devices) for i in range(devices - 1)]
        down = [(j, i) for i, j in up]
        last = lax.slice_in_dim(x, length - width, length, axis=dim)
        first = lax.slice_in_dim(x, 0, width, axis=dim)
        before = lax.ppermute(last, axis, up)
        after = lax.ppermute(first, axis, down)
        x = jnp.concatenate([before, x, after], axis=dim)
    return x


def on_device(cotangent, layer_input, filter_values, weights, row_offset, reach):
    feature_channels, rows, cols = cotangent.shape
    kernels, nlat, span, taps = filter_values.shape
    reach_q = (taps - 1) // 2
    rim = span - 1
    tall = rows + 2 * rim
    first_row = lax.axis_index("lat") * rows
    padded = with_halo(cotangent, (("lat", 1),), rim)
    source = first_row - rim + jnp.arange(tall, dtype=jnp.int32)
    inside = (source >= 0) & (source < nlat)
    safe = jnp.clip(source, 0, nlat - 1)
    offsets = jnp.take(row_offset, safe)
    tap_reach_list = jnp.where(inside, jnp.take(reach, safe), 0)
    psi_rows = jnp.take(filter_values, safe, axis=1).astype(jnp.float32)
    tap_ids = jnp.arange(taps, dtype=jnp.int32) - reach_q
    live = (jnp.abs(tap_ids)[None, :] < tap_reach_list[:, None]).astype(jnp.float32)
    level = (
        jnp.arange(rows, dtype=jnp.int32)[:, None]
        - jnp.arange(tall, dtype=jnp.int32)[None, :]
        + rim
        - offsets[None, :]
    )
    pick = (level[:, :, None] == jnp.arange(span, dtype=jnp.int32)[None, None, :]).astype(
        jnp.float32
    )
    mixing = jnp.einsum("ios,kost->ktio", pick, psi_rows * live[None, :, None, :]).astype(
        jnp.bfloat16
    )
    widest = jnp.max(tap_reach_list)
    lower = reach_q - widest + 1
    upper = reach_q + widest
    moved = lax.all_to_all(padded, "lon", split_axis=0, concat_axis=2, tiled=True)
    wide = jnp.concatenate([moved[:, :, -reach_q:], moved, moved[:, :, :reach_q]], axis=2)
    out_cols = wide.shape[2] - 2 * reach_q
    local_channels = wide.shape[0]

    def add_tap(tap, total):
        shifted = lax.dynamic_slice_in_dim(wide, 2 * reach_q - tap, out_cols, 2)
        mix_tap = lax.dynamic_index_in_dim(mixing, tap, 1, keepdims=False)
        return total + jnp.einsum(
            "kio,col->kcil", mix_tap, shifted, preferred_element_type=jnp.float32
        )

    start = jnp.zeros((kernels, local_channels, rows, out_cols), jnp.float32)
    tap_spread_width = lax.fori_loop(lower, upper, add_tap, start).astype(jnp.bfloat16)
    tap_spread_width = lax.all_to_all(
        tap_spread_width, "lon", split_axis=3, concat_axis=1, tiled=True
    )
    input_grad = lax.dot_general(
        weights, tap_spread_width, (((0, 1), (0, 1)), ((), ())), preferred_element_type=jnp.float32
    )
    partial_grad = lax.dot_general(
        tap_spread_width,
        layer_input,
        (((2, 3), (1, 2)), ((), ())),
        preferred_element_type=jnp.float32,
    )
    total_grad = lax.psum(partial_grad, ("lat", "lon"))
    longitude_count_full = cols * lax.axis_size("lon")
    weight_grad = total_grad / jnp.sqrt(jnp.float32(nlat * longitude_count_full))
    return (input_grad.astype(jnp.bfloat16), weight_grad)


def solution(mesh):
    return jax.shard_map(
        on_device,
        mesh=mesh,
        in_specs=(P(None, "lat", "lon"), P(None, "lat", "lon"), P(), P(), P(), P()),
        out_specs=(P(None, "lat", "lon"), P()),
        check_vma=False,
    )
```

profile of v0, /device:TPU:2, one launch (start us, length us, event | category | flops | bytes accessed | tf_op | source)
XLA Modules:
  0.0 651.0 jit_solution(12407384555351623323)
XLA Ops:
  40.9 13.7 %all-to-all-done = bf16[384,18,128]{2,1,0:T(8,128)(2,1)S(1)} async-done(((bf16[384,18,128]{2,1,0:T(8,128)(2,1)}), bf16[384,18,128]{2,1,0:T(8,128)(2,1)S(1)}, u32[]{:S(2)}, u32[]{:S(2)}) %all-to-all-start) | async-done | bytes 1769504 | tf_op jit(solution)/shard_map/all_to_all | solution.py:51
  70.2 183.5 %while.12 = (s32[]{:T(128)}, f32[3,48,12,1024]{3,2,0,1:T(8,128)}, s32[]{:T(128)}, bf16[48,18,1040]{2,0,1:T(8,128)(2,1)S(1)}, bf16[3,17,12,18]{3,2,0,1:T(8,128)(2...) while((s32[]{:T(128)}, f32[3,48,12,1024]{3,2,0,1:T(8,128)}, s32[]{:T(128)}, ...), condition=%wide.region_2.4_spmd, body=%wide.region_1.3_spmd.sunk | while | flops 65470472 | bytes 21835972 | solution.py:64
  71.0 10.0 %bitcast_add_fusion.2 = f32[3,48,12,1024]{3,2,0,1:T(8,128)} fusion(f32[3,48,12,1024]{3,2,0,1:T(8,128)} %get-tuple-element.167, bf16[48,18,1024]{2,0,1:T(8,128)(2,1)S(1)} %constant_dynamic-slice_fusion.2, bf16[3,17,12,18]{3,2,0,1:T(8,128)(2,1)} %get-tuple-element.180, s32[]{:T(128)S(6)} %select_n.77), kind=kOutput, calls=%fused_computation.3.clone.1 | convolution fusion | flops 65470464 | bytes 18296836 | tf_op jit(solution)/shard_map/while/body/kio,col->kcil/dot_general | solution.py:59
  81.8 10.0 %bitcast_add_fusion.2 = f32[3,48,12,1024]{3,2,0,1:T(8,128)} fusion(f32[3,48,12,1024]{3,2,0,1:T(8,128)} %get-tuple-element.167, bf16[48,18,1024]{2,0,1:T(8,128)(2,1)S(1)} %constant_dynamic-slice_fusion.2, bf16[3,17,12,18]{3,2,0,1:T(8,128)(2,1)} %get-tuple-element.180, s32[]{:T(128)S(6)} %select_n.77), kind=kOutput, calls=%fused_computation.3.clone.1 | convolution fusion | flops 65470464 | bytes 18296836 | tf_op jit(solution)/shard_map/while/body/kio,col->kcil/dot_general | solution.py:59
  92.6 10.0 %bitcast_add_fusion.2 = f32[3,48,12,1024]{3,2,0,1:T(8,128)} fusion(f32[3,48,12,1024]{3,2,0,1:T(8,128)} %get-tuple-element.167, bf16[48,18,1024]{2,0,1:T(8,128)(2,1)S(1)} %constant_dynamic-slice_fusion.2, bf16[3,17,12,18]{3,2,0,1:T(8,128)(2,1)} %get-tuple-element.180, s32[]{:T(128)S(6)} %select_n.77), kind=kOutput, calls=%fused_computation.3.clone.1 | convolution fusion | flops 65470464 | bytes 18296836 | tf_op jit(solution)/shard_map/while/body/kio,col->kcil/dot_general | solution.py:59
  103.4 10.0 %bitcast_add_fusion.2 = f32[3,48,12,1024]{3,2,0,1:T(8,128)} fusion(f32[3,48,12,1024]{3,2,0,1:T(8,128)} %get-tuple-element.167, bf16[48,18,1024]{2,0,1:T(8,128)(2,1)S(1)} %constant_dynamic-slice_fusion.2, bf16[3,17,12,18]{3,2,0,1:T(8,128)(2,1)} %get-tuple-element.180, s32[]{:T(128)S(6)} %select_n.77), kind=kOutput, calls=%fused_computation.3.clone.1 | convolution fusion | flops 65470464 | bytes 18296836 | tf_op jit(solution)/shard_map/while/body/kio,col->kcil/dot_general | solution.py:59
  114.2 10.0 %bitcast_add_fusion.2 = f32[3,48,12,1024]{3,2,0,1:T(8,128)} fusion(f32[3,48,12,1024]{3,2,0,1:T(8,128)} %get-tuple-element.167, bf16[48,18,1024]{2,0,1:T(8,128)(2,1)S(1)} %constant_dynamic-slice_fusion.2, bf16[3,17,12,18]{3,2,0,1:T(8,128)(2,1)} %get-tuple-element.180, s32[]{:T(128)S(6)} %select_n.77), kind=kOutput, calls=%fused_computation.3.clone.1 | convolution fusion | flops 65470464 | bytes 18296836 | tf_op jit(solution)/shard_map/while/body/kio,col->kcil/dot_general | solution.py:59
  125.0 10.0 %bitcast_add_fusion.2 = f32[3,48,12,1024]{3,2,0,1:T(8,128)} fusion(f32[3,48,12,1024]{3,2,0,1:T(8,128)} %get-tuple-element.167, bf16[48,18,1024]{2,0,1:T(8,128)(2,1)S(1)} %constant_dynamic-slice_fusion.2, bf16[3,17,12,18]{3,2,0,1:T(8,128)(2,1)} %get-tuple-element.180, s32[]{:T(128)S(6)} %select_n.77), kind=kOutput, calls=%fused_computation.3.clone.1 | convolution fusion | flops 65470464 | bytes 18296836 | tf_op jit(solution)/shard_map/while/body/kio,col->kcil/dot_general | solution.py:59
  135.8 10.0 %bitcast_add_fusion.2 = f32[3,48,12,1024]{3,2,0,1:T(8,128)} fusion(f32[3,48,12,1024]{3,2,0,1:T(8,128)} %get-tuple-element.167, bf16[48,18,1024]{2,0,1:T(8,128)(2,1)S(1)} %constant_dynamic-slice_fusion.2, bf16[3,17,12,18]{3,2,0,1:T(8,128)(2,1)} %get-tuple-element.180, s32[]{:T(128)S(6)} %select_n.77), kind=kOutput, calls=%fused_computation.3.clone.1 | convolution fusion | flops 65470464 | bytes 18296836 | tf_op jit(solution)/shard_map/while/body/kio,col->kcil/dot_general | solution.py:59
  146.6 10.0 %bitcast_add_fusion.2 = f32[3,48,12,1024]{3,2,0,1:T(8,128)} fusion(f32[3,48,12,1024]{3,2,0,1:T(8,128)} %get-tuple-element.167, bf16[48,18,1024]{2,0,1:T(8,128)(2,1)S(1)} %constant_dynamic-slice_fusion.2, bf16[3,17,12,18]{3,2,0,1:T(8,128)(2,1)} %get-tuple-element.180, s32[]{:T(128)S(6)} %select_n.77), kind=kOutput, calls=%fused_computation.3.clone.1 | convolution fusion | flops 65470464 | bytes 18296836 | tf_op jit(solution)/shard_map/while/body/kio,col->kcil/dot_general | solution.py:59
  157.4 10.0 %bitcast_add_fusion.2 = f32[3,48,12,1024]{3,2,0,1:T(8,128)} fusion(f32[3,48,12,1024]{3,2,0,1:T(8,128)} %get-tuple-element.167, bf16[48,18,1024]{2,0,1:T(8,128)(2,1)S(1)} %constant_dynamic-slice_fusion.2, bf16[3,17,12,18]{3,2,0,1:T(8,128)(2,1)} %get-tuple-element.180, s32[]{:T(128)S(6)} %select_n.77), kind=kOutput, calls=%fused_computation.3.clone.1 | convolution fusion | flops 65470464 | bytes 18296836 | tf_op jit(solution)/shard_map/while/body/kio,col->kcil/dot_general | solution.py:59
  168.1 10.0 %bitcast_add_fusion.2 = f32[3,48,12,1024]{3,2,0,1:T(8,128)} fusion(f32[3,48,12,1024]{3,2,0,1:T(8,128)} %get-tuple-element.167, bf16[48,18,1024]{2,0,1:T(8,128)(2,1)S(1)} %constant_dynamic-slice_fusion.2, bf16[3,17,12,18]{3,2,0,1:T(8,128)(2,1)} %get-tuple-element.180, s32[]{:T(128)S(6)} %select_n.77), kind=kOutput, calls=%fused_computation.3.clone.1 | convolution fusion | flops 65470464 | bytes 18296836 | tf_op jit(solution)/shard_map/while/body/kio,col->kcil/dot_general | solution.py:59
  178.9 10.0 %bitcast_add_fusion.2 = f32[3,48,12,1024]{3,2,0,1:T(8,128)} fusion(f32[3,48,12,1024]{3,2,0,1:T(8,128)} %get-tuple-element.167, bf16[48,18,1024]{2,0,1:T(8,128)(2,1)S(1)} %constant_dynamic-slice_fusion.2, bf16[3,17,12,18]{3,2,0,1:T(8,128)(2,1)} %get-tuple-element.180, s32[]{:T(128)S(6)} %select_n.77), kind=kOutput, calls=%fused_computation.3.clone.1 | convolution fusion | flops 65470464 | bytes 18296836 | tf_op jit(solution)/shard_map/while/body/kio,col->kcil/dot_general | solution.py:59
  189.7 10.0 %bitcast_add_fusion.2 = f32[3,48,12,1024]{3,2,0,1:T(8,128)} fusion(f32[3,48,12,1024]{3,2,0,1:T(8,128)} %get-tuple-element.167, bf16[48,18,1024]{2,0,1:T(8,128)(2,1)S(1)} %constant_dynamic-slice_fusion.2, bf16[3,17,12,18]{3,2,0,1:T(8,128)(2,1)} %get-tuple-element.180, s32[]{:T(128)S(6)} %select_n.77), kind=kOutput, calls=%fused_computation.3.clone.1 | convolution fusion | flops 65470464 | bytes 18296836 | tf_op jit(solution)/shard_map/while/body/kio,col->kcil/dot_general | solution.py:59
  200.5 10.0 %bitcast_add_fusion.2 = f32[3,48,12,1024]{3,2,0,1:T(8,128)} fusion(f32[3,48,12,1024]{3,2,0,1:T(8,128)} %get-tuple-element.167, bf16[48,18,1024]{2,0,1:T(8,128)(2,1)S(1)} %constant_dynamic-slice_fusion.2, bf16[3,17,12,18]{3,2,0,1:T(8,128)(2,1)} %get-tuple-element.180, s32[]{:T(128)S(6)} %select_n.77), kind=kOutput, calls=%fused_computation.3.clone.1 | convolution fusion | flops 65470464 | bytes 18296836 | tf_op jit(solution)/shard_map/while/body/kio,col->kcil/dot_general | solution.py:59
  211.3 10.0 %bitcast_add_fusion.2 = f32[3,48,12,1024]{3,2,0,1:T(8,128)} fusion(f32[3,48,12,1024]{3,2,0,1:T(8,128)} %get-tuple-element.167, bf16[48,18,1024]{2,0,1:T(8,128)(2,1)S(1)} %constant_dynamic-slice_fusion.2, bf16[3,17,12,18]{3,2,0,1:T(8,128)(2,1)} %get-tuple-element.180, s32[]{:T(128)S(6)} %select_n.77), kind=kOutput, calls=%fused_computation.3.clone.1 | convolution fusion | flops 65470464 | bytes 18296836 | tf_op jit(solution)/shard_map/while/body/kio,col->kcil/dot_general | solution.py:59
  222.1 10.0 %bitcast_add_fusion.2 = f32[3,48,12,1024]{3,2,0,1:T(8,128)} fusion(f32[3,48,12,1024]{3,2,0,1:T(8,128)} %get-tuple-element.167, bf16[48,18,1024]{2,0,1:T(8,128)(2,1)S(1)} %constant_dynamic-slice_fusion.2, bf16[3,17,12,18]{3,2,0,1:T(8,128)(2,1)} %get-tuple-element.180, s32[]{:T(128)S(6)} %select_n.77), kind=kOutput, calls=%fused_computation.3.clone.1 | convolution fusion | flops 65470464 | bytes 18296836 | tf_op jit(solution)/shard_map/while/body/kio,col->kcil/dot_general | solution.py:59
  232.9 10.0 %bitcast_add_fusion.2 = f32[3,48,12,1024]{3,2,0,1:T(8,128)} fusion(f32[3,48,12,1024]{3,2,0,1:T(8,128)} %get-tuple-element.167, bf16[48,18,1024]{2,0,1:T(8,128)(2,1)S(1)} %constant_dynamic-slice_fusion.2, bf16[3,17,12,18]{3,2,0,1:T(8,128)(2,1)} %get-tuple-element.180, s32[]{:T(128)S(6)} %select_n.77), kind=kOutput, calls=%fused_computation.3.clone.1 | convolution fusion | flops 65470464 | bytes 18296836 | tf_op jit(solution)/shard_map/while/body/kio,col->kcil/dot_general | solution.py:59
  262.9 14.4 %copy.54 = bf16[3,48,12,1024]{1,2,0,3:T(8,128)(2,1)} copy(bf16[3,48,12,1024]{3,1,2,0:T(8,128)(2,1)} %copy.71) | data formatting | bytes 7077888 | tf_op jit(solution)/shard_map/convert_element_type | solution.py:64
  277.3 16.4 %reshape.127 = bf16[8,2,110592]{2,1,0:T(2,128)(2,1)} reshape(bf16[1024,3,12,48]{3,2,1,0:T(8,128)(2,1)} %bitcast.63) | data formatting | bytes 7077888
  293.8 52.3 %all_to_all.36 = bf16[8,2,110592]{2,1,0:T(2,128)(2,1)} all-to-all(bf16[8,2,110592]{2,1,0:T(2,128)(2,1)} %reshape.127), channel_id=1, replica_groups=mesh['lat'=32,'lon'=8] {'lon'}, dimensions={0} | all-to-all | bytes 7077888 | tf_op jit(solution)/shard_map/all_to_all | solution.py:65
  346.1 17.7 %reshape.128 = bf16[1024,3,12,48]{3,2,1,0:T(8,128)(2,1)} reshape(bf16[8,2,110592]{2,1,0:T(2,128)(2,1)} %all_to_all.36) | data formatting | bytes 7077888
  363.8 13.7 %copy.56 = bf16[3,8,48,12,128]{4,2,1,3,0:T(8,128)(2,1)} copy(bf16[3,8,48,12,128]{2,3,0,4,1:T(8,128)(2,1)} %bitcast.64) | data formatting | bytes 7077888 | tf_op jit(solution)/shard_map/all_to_all | solution.py:65
  388.5 252.8 %all-reduce.2.cloned.1.call-done = f32[3,384,384]{2,1,0:T(8,128)} async-done(((f32[3,384,384]{2,1,0:T(8,128)}), f32[3,384,384]{2,1,0:T(8,128)}) %all-reduce.2.cloned.1.call-update) | async-done | bytes 1769488 | tf_op jit(solution)/shard_map/psum | solution.py:77
  (65 shorter events, 94.5 us)
Async XLA Ops:
  7.2 370.4 %copy-start = (bf16[384,12,128]{2,0,1:T(8,128)(2,1)S(1)}, bf16[384,12,128]{2,0,1:T(8,128)(2,1)}, u32[]{:S(2)}) copy-start(bf16[384,12,128]{2,0,1:T(8,128)(2,1)} %param.11) | copy-start | bytes 3538948
  9.1 5.8 collective-permute-start
  11.5 4.6 collective-permute-start.1
  19.3 7.6 %copy-start.1 = (s32[384]{0:T(512)S(1)}, s32[384]{0:T(512)}, u32[]{:S(2)}) copy-start(s32[384]{0:T(512)} %param.14) | copy-start | bytes 4612
  19.3 8.3 %copy-start.2 = (s32[384]{0:T(512)S(1)}, s32[384]{0:T(512)}, u32[]{:S(2)}) copy-start(s32[384]{0:T(512)} %param.15) | copy-start | bytes 4612
  19.3 35.4 %all-to-all-start = ((bf16[384,18,128]{2,1,0:T(8,128)(2,1)}), bf16[384,18,128]{2,1,0:T(8,128)(2,1)S(1)}, u32[]{:S(2)}, u32[]{:S(2)}) async-start(bf16[384,18,128]{2,1,0:T(8,128)(2,1)} %pad_maximum_fusion), calls=%async_computation | async-start | bytes 4718592 | tf_op jit(solution)/shard_map/all_to_all | solution.py:51
  26.9 614.5 %all-reduce.2.cloned.1.call-start = ((), (), s32[]{:S(2)}) async-start(), calls=%async_computation.2 | async-start | bytes 3538944 | tf_op jit(solution)/shard_map/psum | solution.py:77
  59.7 1.3 copy-start.3
  377.5 5.3 copy-start.4
Sparse Core Ops, SparseCore 0:
  383.0 258.2 all-reduce.1
where the time goes:
time: 653 us; the launch traced here: 651 us
  waiting for transfers between devices  267 us (41%)
  matrix products  181 us (28%)
  local copies, waits for them, and re-layouts  117 us (18%)
  blocking collectives  52.3 us (8%)
  between operations  15.5 us (2%)
  starting transfers between devices  11.3 us (2%)
  other arithmetic  7.17 us (1%)
    psum x1, waiting for transfers between devices, on_device(): total_grad = lax.psum(partial_grad, ('lat', 'lon'))  253 us
    dot_general x17, matrix products, add_tap(): jnp.einsum('kio,col->kcil', mix_tap, shifted, preferred_element_type=jnp....  170 us
    all_to_all x1, blocking collectives, on_device(): lax.all_to_all(tap_spread_width, 'lon', split_axis=3, concat_axis=1, tile...  52.3 us
    unnamed x15, local copies, waits for them, and re-layouts  41 us
    convert_element_type x1, local copies, waits for them, and re-layouts, on_device(): lax.fori_loop(lower, upper, add_tap, start).astype(jnp.bfloat16)  14.4 us
    all_to_all x1, waiting for transfers between devices, on_device(): lax.all_to_all(padded, 'lon', split_axis=0, concat_axis=2, tiled=True)  13.7 us
    all_to_all x1, local copies, waits for them, and re-layouts, on_device(): lax.all_to_all(tap_spread_width, 'lon', split_axis=3, concat_axis=1, tile...  13.7 us
    dynamic_slice x17, local copies, waits for them, and re-layouts, add_tap(): shifted = lax.dynamic_slice_in_dim(wide, 2 * reach_q - tap, out_cols, 2)  13.6 us
  transfers between devices with their start and end apart: 4, of which 2 were waited for; matrix products, arithmetic and copies ran while one was open for 3% of the time, Pallas kernels for 0%

commit v1 on v0

--- a/solution.py
+++ b/solution.py
@@ -62,8 +62,11 @@
 
     start = jnp.zeros((kernels, local_channels, rows, out_cols), jnp.float32)
     tap_spread_width = lax.fori_loop(lower, upper, add_tap, start).astype(jnp.bfloat16)
-    tap_spread_width = lax.all_to_all(
-        tap_spread_width, "lon", split_axis=3, concat_axis=1, tiled=True
+    tap_spread_width = jnp.concatenate(
+        lax.all_to_all(
+            jnp.stack(jnp.split(tap_spread_width, lax.axis_size("lon"), axis=3)), "lon", 0, 0
+        ),
+        axis=1,
     )
     input_grad = lax.dot_general(
         weights, tap_spread_width, (((0, 1), (0, 1)), ((), ())), preferred_element_type=jnp.float32

time: 653 us -> 588 us (0.900)
  local copies, waits for them, and re-layouts: 117 us -> 56.8 us
    unnamed x15 -> x22, local copies, waits for them, and re-layouts: 41 us -> 9.46 us
    convert_element_type x1 -> x0, local copies, waits for them, and re-layouts: 14.4 us -> none  [on_device(): lax.fori_loop(lower, upper, add_tap, start).astype(jnp.bfloat16)]
    all_to_all x1, local copies, waits for them, and re-layouts: 13.7 us -> 0.99 us  [on_device(): lax.all_to_all(jnp.stack(jnp.split(tap_spread_width, lax.axis_size('lon')...]
  transfers between devices with their start and end apart: 4 -> 4, of which waited for: 2 -> 2; matrix products, arithmetic and copies ran while one was open for 3% -> 4% of each run, Pallas kernels for 0% -> 0%
where the time goes in v1:
time: 588 us; the launch traced here: 587 us
  waiting for transfers between devices  266 us (45%)
  matrix products  179 us (30%)
  local copies, waits for them, and re-layouts  56.8 us (10%)
  blocking collectives  50.3 us (9%)
  between operations  15.5 us (3%)
  starting transfers between devices  11.3 us (2%)
  other arithmetic  7.17 us (1%)
    psum x1, waiting for transfers between devices, on_device(): total_grad = lax.psum(partial_grad, ('lat', 'lon'))  253 us
    dot_general x17, matrix products, add_tap(): jnp.einsum('kio,col->kcil', mix_tap, shifted, preferred_element_type=jnp....  170 us
    all_to_all x1, blocking collectives, on_device(): lax.all_to_all(jnp.stack(jnp.split(tap_spread_width, lax.axis_size('lon')...  50.3 us
    all_to_all x1, waiting for transfers between devices, on_device(): lax.all_to_all(padded, 'lon', split_axis=0, concat_axis=2, tiled=True)  13.7 us
    dynamic_slice x17, local copies, waits for them, and re-layouts, add_tap(): shifted = lax.dynamic_slice_in_dim(wide, 2 * reach_q - tap, out_cols, 2)  13.6 us
  transfers between devices with their start and end apart: 4, of which 2 were waited for; matrix products, arithmetic and copies ran while one was open for 4% of the time, Pallas kernels for 0%

profile of v1, /device:TPU:2, one launch (start us, length us, event | category | flops | bytes accessed | tf_op | source)
XLA Modules:
  0.0 586.6 jit_solution(397653686185711014)
XLA Ops:
  19.3 7.6 %all-to-all-start = ((bf16[384,18,128]{2,1,0:T(8,128)(2,1)}), bf16[384,18,128]{2,1,0:T(8,128)(2,1)S(1)}, u32[]{:S(2)}, u32[]{:S(2)}) async-start(bf16[384,18,128]{2,1,0:T(8,128)(2,1)} %pad_maximum_fusion), calls=%async_computation | async-start | bytes 4718592 | tf_op jit(solution)/shard_map/all_to_all | solution.py:51
  40.9 13.7 %all-to-all-done = bf16[384,18,128]{2,1,0:T(8,128)(2,1)S(1)} async-done(((bf16[384,18,128]{2,1,0:T(8,128)(2,1)}), bf16[384,18,128]{2,1,0:T(8,128)(2,1)S(1)}, u32[]{:S(2)}, u32[]{:S(2)}) %all-to-all-start) | async-done | bytes 1769504 | tf_op jit(solution)/shard_map/all_to_all | solution.py:51
  65.4 4.8 broadcast_in_dim.17
  70.2 183.4 %while.12 = (s32[]{:T(128)}, f32[3,48,12,1024]{3,2,0,1:T(8,128)}, s32[]{:T(128)}, bf16[48,18,1040]{2,0,1:T(8,128)(2,1)S(1)}, bf16[3,17,12,18]{3,2,0,1:T(8,128)(2...) while((s32[]{:T(128)}, f32[3,48,12,1024]{3,2,0,1:T(8,128)}, s32[]{:T(128)}, ...), condition=%wide.region_2.4_spmd, body=%wide.region_1.3_spmd.sunk | while | flops 65470472 | bytes 21835972 | solution.py:64
  71.0 10.0 %bitcast_add_fusion.2 = f32[3,48,12,1024]{3,2,0,1:T(8,128)} fusion(f32[3,48,12,1024]{3,2,0,1:T(8,128)} %get-tuple-element.160, bf16[48,18,1024]{2,0,1:T(8,128)(2,1)S(1)} %constant_dynamic-slice_fusion.2, bf16[3,17,12,18]{3,2,0,1:T(8,128)(2,1)} %get-tuple-element.173, s32[]{:T(128)S(6)} %select_n.77), kind=kOutput, calls=%fused_computation.3.clone.1 | convolution fusion | flops 65470464 | bytes 18296836 | tf_op jit(solution)/shard_map/while/body/kio,col->kcil/dot_general | solution.py:59
  81.8 10.0 %bitcast_add_fusion.2 = f32[3,48,12,1024]{3,2,0,1:T(8,128)} fusion(f32[3,48,12,1024]{3,2,0,1:T(8,128)} %get-tuple-element.160, bf16[48,18,1024]{2,0,1:T(8,128)(2,1)S(1)} %constant_dynamic-slice_fusion.2, bf16[3,17,12,18]{3,2,0,1:T(8,128)(2,1)} %get-tuple-element.173, s32[]{:T(128)S(6)} %select_n.77), kind=kOutput, calls=%fused_computation.3.clone.1 | convolution fusion | flops 65470464 | bytes 18296836 | tf_op jit(solution)/shard_map/while/body/kio,col->kcil/dot_general | solution.py:59
  92.6 10.0 %bitcast_add_fusion.2 = f32[3,48,12,1024]{3,2,0,1:T(8,128)} fusion(f32[3,48,12,1024]{3,2,0,1:T(8,128)} %get-tuple-element.160, bf16[48,18,1024]{2,0,1:T(8,128)(2,1)S(1)} %constant_dynamic-slice_fusion.2, bf16[3,17,12,18]{3,2,0,1:T(8,128)(2,1)} %get-tuple-element.173, s32[]{:T(128)S(6)} %select_n.77), kind=kOutput, calls=%fused_computation.3.clone.1 | convolution fusion | flops 65470464 | bytes 18296836 | tf_op jit(solution)/shard_map/while/body/kio,col->kcil/dot_general | solution.py:59
  103.4 10.0 %bitcast_add_fusion.2 = f32[3,48,12,1024]{3,2,0,1:T(8,128)} fusion(f32[3,48,12,1024]{3,2,0,1:T(8,128)} %get-tuple-element.160, bf16[48,18,1024]{2,0,1:T(8,128)(2,1)S(1)} %constant_dynamic-slice_fusion.2, bf16[3,17,12,18]{3,2,0,1:T(8,128)(2,1)} %get-tuple-element.173, s32[]{:T(128)S(6)} %select_n.77), kind=kOutput, calls=%fused_computation.3.clone.1 | convolution fusion | flops 65470464 | bytes 18296836 | tf_op jit(solution)/shard_map/while/body/kio,col->kcil/dot_general | solution.py:59
  114.2 10.0 %bitcast_add_fusion.2 = f32[3,48,12,1024]{3,2,0,1:T(8,128)} fusion(f32[3,48,12,1024]{3,2,0,1:T(8,128)} %get-tuple-element.160, bf16[48,18,1024]{2,0,1:T(8,128)(2,1)S(1)} %constant_dynamic-slice_fusion.2, bf16[3,17,12,18]{3,2,0,1:T(8,128)(2,1)} %get-tuple-element.173, s32[]{:T(128)S(6)} %select_n.77), kind=kOutput, calls=%fused_computation.3.clone.1 | convolution fusion | flops 65470464 | bytes 18296836 | tf_op jit(solution)/shard_map/while/body/kio,col->kcil/dot_general | solution.py:59
  125.0 10.0 %bitcast_add_fusion.2 = f32[3,48,12,1024]{3,2,0,1:T(8,128)} fusion(f32[3,48,12,1024]{3,2,0,1:T(8,128)} %get-tuple-element.160, bf16[48,18,1024]{2,0,1:T(8,128)(2,1)S(1)} %constant_dynamic-slice_fusion.2, bf16[3,17,12,18]{3,2,0,1:T(8,128)(2,1)} %get-tuple-element.173, s32[]{:T(128)S(6)} %select_n.77), kind=kOutput, calls=%fused_computation.3.clone.1 | convolution fusion | flops 65470464 | bytes 18296836 | tf_op jit(solution)/shard_map/while/body/kio,col->kcil/dot_general | solution.py:59
  135.7 10.0 %bitcast_add_fusion.2 = f32[3,48,12,1024]{3,2,0,1:T(8,128)} fusion(f32[3,48,12,1024]{3,2,0,1:T(8,128)} %get-tuple-element.160, bf16[48,18,1024]{2,0,1:T(8,128)(2,1)S(1)} %constant_dynamic-slice_fusion.2, bf16[3,17,12,18]{3,2,0,1:T(8,128)(2,1)} %get-tuple-element.173, s32[]{:T(128)S(6)} %select_n.77), kind=kOutput, calls=%fused_computation.3.clone.1 | convolution fusion | flops 65470464 | bytes 18296836 | tf_op jit(solution)/shard_map/while/body/kio,col->kcil/dot_general | solution.py:59
  146.5 10.0 %bitcast_add_fusion.2 = f32[3,48,12,1024]{3,2,0,1:T(8,128)} fusion(f32[3,48,12,1024]{3,2,0,1:T(8,128)} %get-tuple-element.160, bf16[48,18,1024]{2,0,1:T(8,128)(2,1)S(1)} %constant_dynamic-slice_fusion.2, bf16[3,17,12,18]{3,2,0,1:T(8,128)(2,1)} %get-tuple-element.173, s32[]{:T(128)S(6)} %select_n.77), kind=kOutput, calls=%fused_computation.3.clone.1 | convolution fusion | flops 65470464 | bytes 18296836 | tf_op jit(solution)/shard_map/while/body/kio,col->kcil/dot_general | solution.py:59
  157.3 10.0 %bitcast_add_fusion.2 = f32[3,48,12,1024]{3,2,0,1:T(8,128)} fusion(f32[3,48,12,1024]{3,2,0,1:T(8,128)} %get-tuple-element.160, bf16[48,18,1024]{2,0,1:T(8,128)(2,1)S(1)} %constant_dynamic-slice_fusion.2, bf16[3,17,12,18]{3,2,0,1:T(8,128)(2,1)} %get-tuple-element.173, s32[]{:T(128)S(6)} %select_n.77), kind=kOutput, calls=%fused_computation.3.clone.1 | convolution fusion | flops 65470464 | bytes 18296836 | tf_op jit(solution)/shard_map/while/body/kio,col->kcil/dot_general | solution.py:59
  168.1 10.0 %bitcast_add_fusion.2 = f32[3,48,12,1024]{3,2,0,1:T(8,128)} fusion(f32[3,48,12,1024]{3,2,0,1:T(8,128)} %get-tuple-element.160, bf16[48,18,1024]{2,0,1:T(8,128)(2,1)S(1)} %constant_dynamic-slice_fusion.2, bf16[3,17,12,18]{3,2,0,1:T(8,128)(2,1)} %get-tuple-element.173, s32[]{:T(128)S(6)} %select_n.77), kind=kOutput, calls=%fused_computation.3.clone.1 | convolution fusion | flops 65470464 | bytes 18296836 | tf_op jit(solution)/shard_map/while/body/kio,col->kcil/dot_general | solution.py:59
  178.9 10.0 %bitcast_add_fusion.2 = f32[3,48,12,1024]{3,2,0,1:T(8,128)} fusion(f32[3,48,12,1024]{3,2,0,1:T(8,128)} %get-tuple-element.160, bf16[48,18,1024]{2,0,1:T(8,128)(2,1)S(1)} %constant_dynamic-slice_fusion.2, bf16[3,17,12,18]{3,2,0,1:T(8,128)(2,1)} %get-tuple-element.173, s32[]{:T(128)S(6)} %select_n.77), kind=kOutput, calls=%fused_computation.3.clone.1 | convolution fusion | flops 65470464 | bytes 18296836 | tf_op jit(solution)/shard_map/while/body/kio,col->kcil/dot_general | solution.py:59
  189.7 10.0 %bitcast_add_fusion.2 = f32[3,48,12,1024]{3,2,0,1:T(8,128)} fusion(f32[3,48,12,1024]{3,2,0,1:T(8,128)} %get-tuple-element.160, bf16[48,18,1024]{2,0,1:T(8,128)(2,1)S(1)} %constant_dynamic-slice_fusion.2, bf16[3,17,12,18]{3,2,0,1:T(8,128)(2,1)} %get-tuple-element.173, s32[]{:T(128)S(6)} %select_n.77), kind=kOutput, calls=%fused_computation.3.clone.1 | convolution fusion | flops 65470464 | bytes 18296836 | tf_op jit(solution)/shard_map/while/body/kio,col->kcil/dot_general | solution.py:59
  200.5 10.0 %bitcast_add_fusion.2 = f32[3,48,12,1024]{3,2,0,1:T(8,128)} fusion(f32[3,48,12,1024]{3,2,0,1:T(8,128)} %get-tuple-element.160, bf16[48,18,1024]{2,0,1:T(8,128)(2,1)S(1)} %constant_dynamic-slice_fusion.2, bf16[3,17,12,18]{3,2,0,1:T(8,128)(2,1)} %get-tuple-element.173, s32[]{:T(128)S(6)} %select_n.77), kind=kOutput, calls=%fused_computation.3.clone.1 | convolution fusion | flops 65470464 | bytes 18296836 | tf_op jit(solution)/shard_map/while/body/kio,col->kcil/dot_general | solution.py:59
  211.3 10.0 %bitcast_add_fusion.2 = f32[3,48,12,1024]{3,2,0,1:T(8,128)} fusion(f32[3,48,12,1024]{3,2,0,1:T(8,128)} %get-tuple-element.160, bf16[48,18,1024]{2,0,1:T(8,128)(2,1)S(1)} %constant_dynamic-slice_fusion.2, bf16[3,17,12,18]{3,2,0,1:T(8,128)(2,1)} %get-tuple-element.173, s32[]{:T(128)S(6)} %select_n.77), kind=kOutput, calls=%fused_computation.3.clone.1 | convolution fusion | flops 65470464 | bytes 18296836 | tf_op jit(solution)/shard_map/while/body/kio,col->kcil/dot_general | solution.py:59
  222.1 10.0 %bitcast_add_fusion.2 = f32[3,48,12,1024]{3,2,0,1:T(8,128)} fusion(f32[3,48,12,1024]{3,2,0,1:T(8,128)} %get-tuple-element.160, bf16[48,18,1024]{2,0,1:T(8,128)(2,1)S(1)} %constant_dynamic-slice_fusion.2, bf16[3,17,12,18]{3,2,0,1:T(8,128)(2,1)} %get-tuple-element.173, s32[]{:T(128)S(6)} %select_n.77), kind=kOutput, calls=%fused_computation.3.clone.1 | convolution fusion | flops 65470464 | bytes 18296836 | tf_op jit(solution)/shard_map/while/body/kio,col->kcil/dot_general | solution.py:59
  232.9 10.0 %bitcast_add_fusion.2 = f32[3,48,12,1024]{3,2,0,1:T(8,128)} fusion(f32[3,48,12,1024]{3,2,0,1:T(8,128)} %get-tuple-element.160, bf16[48,18,1024]{2,0,1:T(8,128)(2,1)S(1)} %constant_dynamic-slice_fusion.2, bf16[3,17,12,18]{3,2,0,1:T(8,128)(2,1)} %get-tuple-element.173, s32[]{:T(128)S(6)} %select_n.77), kind=kOutput, calls=%fused_computation.3.clone.1 | convolution fusion | flops 65470464 | bytes 18296836 | tf_op jit(solution)/shard_map/while/body/kio,col->kcil/dot_general | solution.py:59
  243.6 10.0 %bitcast_add_fusion.2 = f32[3,48,12,1024]{3,2,0,1:T(8,128)} fusion(f32[3,48,12,1024]{3,2,0,1:T(8,128)} %get-tuple-element.160, bf16[48,18,1024]{2,0,1:T(8,128)(2,1)S(1)} %constant_dynamic-slice_fusion.2, bf16[3,17,12,18]{3,2,0,1:T(8,128)(2,1)} %get-tuple-element.173, s32[]{:T(128)S(6)} %select_n.77), kind=kOutput, calls=%fused_computation.3.clone.1 | convolution fusion | flops 65470464 | bytes 18296836 | tf_op jit(solution)/shard_map/while/body/kio,col->kcil/dot_general | solution.py:59
  253.6 7.4 %copy.60 = bf16[3,48,12,1024]{3,1,2,0:T(8,128)(2,1)S(1)} copy(f32[3,48,12,1024]{3,2,0,1:T(8,128)} %get-tuple-element.71) | data formatting | bytes 10616832 | tf_op jit(solution)/shard_map/while | solution.py:64
  262.3 50.3 %all_to_all.23 = bf16[8,3,48,12,128]{4,2,3,1,0:T(8,128)(2,1)S(1)} all-to-all(bf16[8,3,48,12,128]{4,2,3,1,0:T(8,128)(2,1)S(1)} %fusion.7), channel_id=1, replica_groups=mesh['lat'=32,'lon'=8] {'lon'}, dimensions={0} | all-to-all | bytes 7077888 | tf_op jit(solution)/shard_map/all_to_all | solution.py:66
  324.2 252.7 %all-reduce.2.cloned.1.call-done = f32[3,384,384]{2,1,0:T(8,128)} async-done(((f32[3,384,384]{2,1,0:T(8,128)}), f32[3,384,384]{2,1,0:T(8,128)}) %all-reduce.2.cloned.1.call-update) | async-done | bytes 1769488 | tf_op jit(solution)/shard_map/psum | solution.py:80
  (72 shorter events, 64.7 us)
Async XLA Ops:
  7.2 308.2 %copy-start = (bf16[384,12,128]{2,0,1:T(8,128)(2,1)S(1)}, bf16[384,12,128]{2,0,1:T(8,128)(2,1)}, u32[]{:S(2)}) copy-start(bf16[384,12,128]{2,0,1:T(8,128)(2,1)} %param.11) | copy-start | bytes 3538948
  9.1 5.8 collective-permute-start
  11.5 4.6 collective-permute-start.1
  19.3 7.6 %copy-start.1 = (s32[384]{0:T(512)S(1)}, s32[384]{0:T(512)}, u32[]{:S(2)}) copy-start(s32[384]{0:T(512)} %param.14) | copy-start | bytes 4612
  19.3 8.3 %copy-start.2 = (s32[384]{0:T(512)S(1)}, s32[384]{0:T(512)}, u32[]{:S(2)}) copy-start(s32[384]{0:T(512)} %param.15) | copy-start | bytes 4612
  19.3 35.4 %all-to-all-start = ((bf16[384,18,128]{2,1,0:T(8,128)(2,1)}), bf16[384,18,128]{2,1,0:T(8,128)(2,1)S(1)}, u32[]{:S(2)}, u32[]{:S(2)}) async-start(bf16[384,18,128]{2,1,0:T(8,128)(2,1)} %pad_maximum_fusion), calls=%async_computation | async-start | bytes 4718592 | tf_op jit(solution)/shard_map/all_to_all | solution.py:51
  26.9 550.0 %all-reduce.2.cloned.1.call-start = ((), (), s32[]{:S(2)}) async-start(), calls=%async_computation.2 | async-start | bytes 3538944 | tf_op jit(solution)/shard_map/psum | solution.py:80
  59.7 1.3 copy-start.4
  313.6 1.7 copy-start.3
  315.3 3.3 copy-start.5
Sparse Core Ops, SparseCore 0:
  318.7 258.1 all-reduce.1
